TPU v7x, 32 devices: a whole 2x2x4 slice. The times are simulated.
32 devices in a mesh: groups: 2 (over x), row: 8 (over z, y), col: 2 (over core).
Axes of the slice: x: 2, y: 2, z: 4, core: 2. Of those that a mesh axis runs over, the one named last changes fastest.
Arguments:
- features: bfloat16 [32, 8, 256, 1024], P(('groups', 'row'), 'col'), parts along dimension 0, may hold values from -6 to 6
- assignment: int32 [32, 8], P(('groups', 'row'), 'col'), parts along dimension 0, may hold values from -1 to 7, as said below
- w_reduce: bfloat16 [1024, 512], replicated, may hold values from -0.1875 to 0.1875
- w_expand: bfloat16 [512, 2048], replicated, may hold values from -0.25 to 0.25
- w_short: bfloat16 [1024, 2048], replicated, may hold values from -0.1875 to 0.1875
- w_branch: bfloat16 [2048, 256], replicated, may hold values from -0.125 to 0.125
- w_dilated: bfloat16 [9, 256, 256], replicated, may hold values from -0.125 to 0.125
Outputs:
- branch_out: bfloat16 [512, 128, 256], P(('groups', 'row'), 'col'), parts along dimension 0
There are 2 independent parts, one for each index of `groups`. A program takes and returns all parts, laid end to end along the dimension named above; an argument that names none is the same for every part. Nothing has to cross between parts.
Inputs may be any that keep to these rules, and one draw needn't show every extreme that they name: `assignment`: A value v >= 0 means the tile has tissue and is handled in slot v % 4 by the worker of the same column index whose row index is the holder's row index XOR (v // 4): the holder itself for v < 4, else its partner. Each worker handles exactly 4 tiles, one in each slot, the holder's own tissue tiles included. In every column index some device's tiles are all tissue, so that it hands 4 tiles to its partner, and that partner holds none.
All inputs are finite; a program needn't handle non-finite values.
Results may differ from a plain program's by a relative error of at most 0.0061.
Values may be sent and summed in bfloat16 or wider, within the bound.
A program may use at most 64 MiB of HBM per device.

v0:
```python
import jax
import jax.numpy as jnp
from jax import lax
from jax.sharding import PartitionSpec as P

TILE = 16
RR = 18
RC = 15


def extended_2(cells, sides, width):
    for axis, dim in sides:
        count = lax.axis_size(axis)
        ends = count - 1
        head = lax.slice_in_dim(cells, 0, width, axis=dim)
        tail = lax.slice_in_dim(cells, cells.shape[dim] - width, cells.shape[dim], axis=dim)
        cells = jnp.concatenate(
            [
                lax.ppermute(tail, axis, [(i, (i + 1) % count) for i in range(ends)]),
                cells,
                lax.ppermute(head, axis, [((i + 1) % count, i) for i in range(ends)]),
            ],
            axis=dim,
        )
    return cells


def trunk(rows_in, w_reduce, w_expand, w_short, w_branch):
    hidden = jax.nn.relu(jnp.dot(rows_in, w_reduce, preferred_element_type=jnp.float32)).astype(
        jnp.bfloat16
    )
    summed = jnp.dot(hidden, w_expand, preferred_element_type=jnp.float32) + jnp.dot(
        rows_in, w_short, preferred_element_type=jnp.float32
    )
    block_out = jax.nn.relu(summed).astype(jnp.bfloat16)
    return jax.nn.relu(jnp.dot(block_out, w_branch, preferred_element_type=jnp.float32)).astype(
        jnp.bfloat16
    )


def shards(features, assignment, w_reduce, w_expand, w_short, w_branch, w_dilated):
    tile_rows, tile_cols, pixels, channels = features.shape
    tile_count = tile_rows * tile_cols
    branch_width = w_branch.shape[1]
    flat_in = features.reshape(tile_count, pixels * channels)
    tile_codes = assignment.reshape(tile_count)
    tissue = tile_codes >= 0
    reduced = trunk(
        flat_in.reshape(tile_count * pixels, channels), w_reduce, w_expand, w_short, w_branch
    )
    reduced = reduced.reshape(tile_count, pixels * branch_width)
    reduced = jnp.where(tissue[:, None], reduced, jnp.zeros_like(reduced))
    height = tile_rows * TILE
    width = tile_cols * TILE
    feature_grid = (
        reduced.reshape(tile_rows, tile_cols, TILE, TILE, branch_width)
        .transpose(0, 2, 1, 3, 4)
        .reshape(height, width, branch_width)
    )
    extended = extended_2(feature_grid, (("row", 0),), RR)
    extended = extended_2(extended, (("col", 1),), RC)
    col_margin = (extended.shape[1] - width) // 2
    windows = []
    for down_tap in range(3):
        for side_tap in range(3):
            col_start = col_margin - RC + side_tap * RC
            window = extended[down_tap * RR : down_tap * RR + height, col_start : col_start + width]
            windows.append(window.reshape(height * width, branch_width))
    stacked = jnp.concatenate(windows, axis=1)
    summed = jnp.dot(
        stacked,
        w_dilated.reshape(9 * branch_width, branch_width),
        preferred_element_type=jnp.float32,
    )
    return jax.nn.relu(summed).astype(jnp.bfloat16).reshape(height, width, branch_width)


def solution(mesh):
    in_specs = (
        P(("groups", "row"), "col", None, None),
        P(("groups", "row"), "col"),
        P(),
        P(),
        P(),
        P(),
        P(),
    )
    out_specs = P(("groups", "row"), "col", None)
    return jax.shard_map(shards, mesh=mesh, in_specs=in_specs, out_specs=out_specs, check_vma=False)
```

profile of v0, /device:TPU:25, one launch (start us, length us, event | category | flops | bytes accessed | tf_op | source)
XLA Modules:
  0.0 79.6 jit_solution(9862306816485134618)
XLA Ops:
  0.0 0.8 %broadcast_compare_fusion = pred[2,4]{1,0:T(4,128)(4,1)S(1)} fusion(s32[2,4]{1,0:T(2,128)} %param.8), kind=kLoop, calls=%fused_computation.27 | loop fusion | flops 8 | bytes 40 | tf_op jit(solution)/shard_map/ge | solution.py:47
  0.8 0.8 copy-done
  1.6 12.0 %fusion.7 = f32[2048,2048]{1,0:T(8,128)} fusion(bf16[512,2048]{1,0:T(8,128)(2,1)S(1)} %copy-done, bf16[2048,1024]{1,0:T(8,128)(2,1)} %bitcast.39, bf16[1024,512]{1,0:T(8,128)(2,1)} %param.9), kind=kOutput, calls=%fused_computation.14 | convolution fusion | flops 6444548096 | bytes 24117248 | tf_op jit(solution)/shard_map/dot_general | solution.py:32
  13.6 19.7 %fusion.6 = bf16[2048,256]{1,0:T(8,128)(2,1)S(1)} fusion(bf16[2048,256]{1,0:T(8,128)(2,1)} %param.12, f32[2048,2048]{1,0:T(8,128)} %fusion.7, bf16[2048,1024]{1,0:T(8,128)(2,1)} %bitcast.40, bf16[1024,2048]{1,0:T(8,128)(2,1)} %param.11), kind=kOutput, calls=%fused_computation.10 | convolution fusion | flops 10751049728 | bytes 27262976 | tf_op jit(solution)/shard_map/dot_general | solution.py:36
  33.2 0.1 copy_select_fusion
  33.4 0.1 fusion.12
  33.5 3.1 %collective-permute-start = (bf16[18,64,256]{2,1,0:T(8,128)(2,1)S(1)}, bf16[18,64,256]{2,1,0:T(8,128)(2,1)S(1)}, u32[]{:S(2)}, u32[]{:S(2)}) collective-permute-start(bf16[18,64,256]{2,1,0:T(8,128)(2,1)S(1)} %get-tuple-element.17), channel_id=1, source_target_pairs={{0,2},{2,4},{4,6},{6,8},{8,10},{10,12},{12,14},{1,3},{3,5},{5,7},{... | collective-permute-start | bytes 1769480 | tf_op jit(solution)/shard_map/ppermute | solution.py:19
  36.6 3.1 %collective-permute-start.1 = (bf16[18,64,256]{2,1,0:T(8,128)(2,1)S(1)}, bf16[18,64,256]{2,1,0:T(8,128)(2,1)S(1)}, u32[]{:S(2)}, u32[]{:S(2)}) collective-permute-start(bf16[18,64,256]{2,1,0:T(8,128)(2,1)S(1)} %get-tuple-element.18), channel_id=1, source_target_pairs={{2,0},{4,2},{6,4},{8,6},{10,8},{12,10},{14,12},{3,1},{5,3},{7,5},{... | collective-permute-start | bytes 1769480 | tf_op jit(solution)/shard_map/ppermute | solution.py:21
  39.7 10.9 %collective-permute-done = bf16[18,64,256]{2,1,0:T(8,128)(2,1)S(1)} collective-permute-done((bf16[18,64,256]{2,1,0:T(8,128)(2,1)S(1)}, bf16[18,64,256]{2,1,0:T(8,128)(2,1)S(1)}, u32[]{:S(2)}, u32[]{:S(2)}) %collective-permute-start) | collective-permute-done | bytes 589856 | tf_op jit(solution)/shard_map/ppermute | solution.py:19
  50.6 13.6 %collective-permute-done.1 = bf16[18,64,256]{2,1,0:T(8,128)(2,1)S(1)} collective-permute-done((bf16[18,64,256]{2,1,0:T(8,128)(2,1)S(1)}, bf16[18,64,256]{2,1,0:T(8,128)(2,1)S(1)}, u32[]{:S(2)}, u32[]{:S(2)}) %collective-permute-start.1) | collective-permute-done | bytes 589856 | tf_op jit(solution)/shard_map/ppermute | solution.py:21
  64.2 0.2 pad_maximum_fusion.3
  64.4 0.2 copy.10
  64.6 1.3 %collective-permute-start.2 = (bf16[68,15,256]{2,0,1:T(8,128)(2,1)S(1)}, bf16[68,15,256]{2,0,1:T(8,128)(2,1)S(1)}, u32[]{:S(2)}, u32[]{:S(2)}) collective-permute-start(bf16[68,15,256]{2,0,1:T(8,128)(2,1)S(1)} %copy.10), channel_id=1, source_target_pairs={{0,1},{2,3},{4,5},{6,7},{8,9},{10,11},{12,13},{14,15},{16,17},{18,... | collective-permute-start | bytes 1566728 | tf_op jit(solution)/shard_map/ppermute | solution.py:19
  65.9 0.2 copy.12
  66.1 3.1 %collective-permute-start.3 = (bf16[68,15,256]{2,0,1:T(8,128)(2,1)S(1)}, bf16[68,15,256]{2,0,1:T(8,128)(2,1)S(1)}, u32[]{:S(2)}, u32[]{:S(2)}) collective-permute-start(bf16[68,15,256]{2,0,1:T(8,128)(2,1)S(1)} %copy.12), channel_id=1, source_target_pairs={{1,0},{3,2},{5,4},{7,6},{9,8},{11,10},{13,12},{15,14},{17,16},{19,... | collective-permute-start | bytes 1566728 | tf_op jit(solution)/shard_map/ppermute | solution.py:21
  69.2 0.2 pad_maximum_fusion.1
  69.4 0.1 copy.11
  69.5 1.2 %collective-permute-done.3 = bf16[68,15,256]{2,0,1:T(8,128)(2,1)S(1)} collective-permute-done((bf16[68,15,256]{2,0,1:T(8,128)(2,1)S(1)}, bf16[68,15,256]{2,0,1:T(8,128)(2,1)S(1)}, u32[]{:S(2)}, u32[]{:S(2)}) %collective-permute-start.3) | collective-permute-done | bytes 522272 | tf_op jit(solution)/shard_map/ppermute | solution.py:21
  70.7 0.1 copy.13
  70.8 1.9 %pad_maximum_fusion = (bf16[68,79,256]{2,1,0:T(8,128)(2,1)S(1)}, bf16[68,79,256]{2,1,0:T(8,128)(2,1)S(1)}) fusion(bf16[68,15,256]{2,1,0:T(8,128)(2,1)S(1)} %copy.13, bf16[18,64,256]{2,1,0:T(8,128)(2,1)S(1)} %collective-permute-done.1, bf16[32,64,256]{2,1,0:T(8,128)(2,1)S(1)} %bitcast.28, bf16[18,64,256]{2,1,0:T(8,128)(2,1)S(1)} %collective-permute-done, ...), kind=kLoop, calls=%fused_computation.6 | loop fusion | flops 22003712 | bytes 8773632 | tf_op jit(solution)/shard_map/concatenate | solution.py:17
  72.7 1.5 %fusion.10 = (bf16[32,64,256]{2,1,0:T(8,128)(2,1)S(1)}, bf16[32,64,256]{2,1,0:T(8,128)(2,1)S(1)}, bf16[32,64,256]{2,1,0:T(8,128)(2,1)S(1)}, bf16[32,64,256]{2,1,...) fusion(bf16[68,79,256]{2,1,0:T(8,128)(2,1)S(1)} %get-tuple-element.11, ...), kind=kLoop, calls=%fused_computation.30 | loop fusion | bytes 12582912 | tf_op jit(solution)/shard_map/slice | solution.py:67
  74.3 0.1 constant_dynamic-update-slice_fusion.7
  74.9 0.9 %copy-done.1 = bf16[9,256,256]{2,1,0:T(8,128)(2,1)S(1)} copy-done((bf16[9,256,256]{2,1,0:T(8,128)(2,1)S(1)}, bf16[9,256,256]{2,1,0:T(8,128)(2,1)}, u32[]{:S(2)}) %copy-start.1) | copy-done | bytes 1179672
  75.9 3.7 %fusion.5 = bf16[2048,256]{1,0:T(8,128)(2,1)} fusion(bf16[2048,2304]{1,0:T(8,128)(2,1)S(1)} %constant_dynamic-update-slice_fusion, bf16[2304,256]{1,0:T(8,128)(2,1)S(1)} %bitcast.41), kind=kOutput, calls=%fused_computation.9 | convolution fusion | flops 2416967680 | bytes 11665408 | tf_op jit(solution)/shard_map/dot_general | solution.py:70
  (11 shorter events, 0.6 us)
Async XLA Ops:
  0.0 1.6 %copy-start = (bf16[512,2048]{1,0:T(8,128)(2,1)S(1)}, bf16[512,2048]{1,0:T(8,128)(2,1)}, u32[]{:S(2)}) copy-start(bf16[512,2048]{1,0:T(8,128)(2,1)} %param.10) | copy-start | bytes 6291460
  33.5 17.0 %collective-permute-start = (bf16[18,64,256]{2,1,0:T(8,128)(2,1)S(1)}, bf16[18,64,256]{2,1,0:T(8,128)(2,1)S(1)}, u32[]{:S(2)}, u32[]{:S(2)}) collective-permute-start(bf16[18,64,256]{2,1,0:T(8,128)(2,1)S(1)} %get-tuple-element.17), channel_id=1, source_target_pairs={{0,2},{2,4},{4,6},{6,8},{8,10},{10,12},{12,14},{1,3},{3,5},{5,7},{... | collective-permute-start | bytes 1769480 | tf_op jit(solution)/shard_map/ppermute | solution.py:19
  36.6 27.5 %collective-permute-start.1 = (bf16[18,64,256]{2,1,0:T(8,128)(2,1)S(1)}, bf16[18,64,256]{2,1,0:T(8,128)(2,1)S(1)}, u32[]{:S(2)}, u32[]{:S(2)}) collective-permute-start(bf16[18,64,256]{2,1,0:T(8,128)(2,1)S(1)} %get-tuple-element.18), channel_id=1, source_target_pairs={{2,0},{4,2},{6,4},{8,6},{10,8},{12,10},{14,12},{3,1},{5,3},{7,5},{... | collective-permute-start | bytes 1769480 | tf_op jit(solution)/shard_map/ppermute | solution.py:21
  64.6 4.8 %collective-permute-start.2 = (bf16[68,15,256]{2,0,1:T(8,128)(2,1)S(1)}, bf16[68,15,256]{2,0,1:T(8,128)(2,1)S(1)}, u32[]{:S(2)}, u32[]{:S(2)}) collective-permute-start(bf16[68,15,256]{2,0,1:T(8,128)(2,1)S(1)} %copy.10), channel_id=1, source_target_pairs={{0,1},{2,3},{4,5},{6,7},{8,9},{10,11},{12,13},{14,15},{16,17},{18,... | collective-permute-start | bytes 1566728 | tf_op jit(solution)/shard_map/ppermute | solution.py:19
  66.1 4.6 %collective-permute-start.3 = (bf16[68,15,256]{2,0,1:T(8,128)(2,1)S(1)}, bf16[68,15,256]{2,0,1:T(8,128)(2,1)S(1)}, u32[]{:S(2)}, u32[]{:S(2)}) collective-permute-start(bf16[68,15,256]{2,0,1:T(8,128)(2,1)S(1)} %copy.12), channel_id=1, source_target_pairs={{1,0},{3,2},{5,4},{7,6},{9,8},{11,10},{13,12},{15,14},{17,16},{19,... | collective-permute-start | bytes 1566728 | tf_op jit(solution)/shard_map/ppermute | solution.py:21
  74.6 1.3 %copy-start.1 = (bf16[9,256,256]{2,1,0:T(8,128)(2,1)S(1)}, bf16[9,256,256]{2,1,0:T(8,128)(2,1)}, u32[]{:S(2)}) copy-start(bf16[9,256,256]{2,1,0:T(8,128)(2,1)} %param.13) | copy-start | bytes 3538948
where the time goes:
time: 79.8 us; the launch traced here: 79.6 us
  matrix products  35.3 us (44%)
  waiting for transfers between devices  25.7 us (32%)
  starting transfers between devices  10.6 us (13%)
  local copies, waits for them, and re-layouts  4.53 us (6%)
  other arithmetic  3.25 us (4%)
    dot_general x1, matrix products, trunk(): jnp.dot(block_out, w_branch, preferred_element_type=jnp.float32)  19.7 us
    ppermute x2, waiting for transfers between devices, extended_2(): lax.ppermute(head, axis, [((i + 1) % count, i) for i in range(ends)])  14.8 us
    dot_general x1, matrix products, trunk(): jnp.dot(hidden, w_expand, preferred_element_type=jnp.float32)  12 us
    ppermute x2, waiting for transfers between devices, extended_2(): lax.ppermute(tail, axis, [(i, (i + 1) % count) for i in range(ends)])  10.9 us
    ppermute x2, starting transfers between devices, extended_2(): lax.ppermute(head, axis, [((i + 1) % count, i) for i in range(ends)])  6.15 us
    ppermute x2, starting transfers between devices, extended_2(): lax.ppermute(tail, axis, [(i, (i + 1) % count) for i in range(ends)])  4.42 us
    dot_general x1, matrix products, shards(): jnp.dot(stacked, w_dilated.reshape(9 * branch_width, branch_width), prefe...  3.69 us
    unnamed x12, local copies, waits for them, and re-layouts  2.29 us
  transfers between devices with their start and end apart: 4, of which 3 were waited for; matrix products, arithmetic and copies ran while one was open for 1% of the time, Pallas kernels for 0%

commit v1 on v0

v1 whole, which is shorter than its diff:
```python
import functools

import jax
import jax.numpy as jnp
from jax import lax
from jax.experimental import pallas as pl
from jax.experimental.pallas import tpu as pltpu
from jax.sharding import PartitionSpec as P

TILE = 16
RR = 18
RC = 15
MESH = pl.DeviceIdType.MESH


def kernel(
    row_count, col_count,
    codes, features, w_reduce, w_expand, w_short, w_branch, w_dilated, out,
    xh, v_reduce, v_cat, v_branch, v_dilated, block, grid, stacked, acc, out_buf,
    x_sem, w_sem, out_sem, row_send, row_recv, col_send, col_recv,
):
    tile_rows, tile_cols, pixels, channels = features.shape
    mid = w_reduce.shape[1]
    cout = w_expand.shape[1]
    width = w_branch.shape[1]
    height = tile_rows * TILE
    row = lax.axis_index("row")
    col = lax.axis_index("col")
    has_up = row > 0
    has_down = row < row_count - 1
    has_left = col > 0
    has_right = col < col_count - 1
    sides = ((has_up, {"row": row - 1}), (has_down, {"row": row + 1}),
             (has_left, {"col": col - 1}), (has_right, {"col": col + 1}))

    def tile_col(step):
        return jnp.where(col == 0, tile_cols - 1 - step, step)

    def x_copy(tile_row, step):
        return pltpu.make_async_copy(
            features.at[tile_row, tile_col(step)],
            xh.at[tile_row, step, :, pl.ds(0, channels)],
            x_sem.at[tile_row, step],
        )

    last = tile_rows - 1
    reduce_copy = pltpu.make_async_copy(w_reduce, v_reduce, w_sem.at[0])
    short_copy = pltpu.make_async_copy(w_short, v_cat.at[pl.ds(0, channels)], w_sem.at[1])
    expand_copy = pltpu.make_async_copy(w_expand, v_cat.at[pl.ds(channels, mid)], w_sem.at[2])
    branch_copy = pltpu.make_async_copy(w_branch, v_branch, w_sem.at[3])
    dilated_copy = pltpu.make_async_copy(w_dilated, v_dilated, w_sem.at[4])
    x_copy(last, 0).start()
    reduce_copy.start()
    short_copy.start()
    expand_copy.start()
    branch_copy.start()
    for tile_row in reversed(range(last)):
        x_copy(tile_row, 0).start()
    for step in range(1, tile_cols):
        for tile_row in reversed(range(tile_rows)):
            x_copy(tile_row, step).start()
    dilated_copy.start()

    barrier = pltpu.get_barrier_semaphore()
    for there, device in sides:
        @pl.when(there)
        def _(device=device):
            pl.semaphore_signal(barrier, inc=1, device_id=device, device_id_type=MESH)

    @pl.when(jnp.logical_not(has_up))
    def _():
        grid[0:RR] = jnp.zeros((RR,) + grid.shape[1:], grid.dtype)

    @pl.when(jnp.logical_not(has_down))
    def _():
        grid[RR + height:] = jnp.zeros((RR,) + grid.shape[1:], grid.dtype)

    @pl.when(jnp.logical_not(has_left))
    def _():
        grid[:, 0] = jnp.zeros((grid.shape[0],) + grid.shape[2:], grid.dtype)

    @pl.when(jnp.logical_not(has_right))
    def _():
        grid[:, tile_cols + 1] = jnp.zeros((grid.shape[0],) + grid.shape[2:], grid.dtype)

    strip = RR - TILE

    def row_copy(kind, step):
        at = tile_col(step) + 1
        if kind == 0:
            src, dst, size, device = height + RR - TILE, strip, TILE, {"row": row + 1}
        elif kind == 1:
            src, dst, size, device = height, 0, strip, {"row": row + 1}
        else:
            src, dst, size, device = RR, RR + height, RR, {"row": row - 1}
        return pltpu.make_async_remote_copy(
            src_ref=grid.at[pl.ds(src, size), at],
            dst_ref=grid.at[pl.ds(dst, size), at],
            send_sem=row_send.at[kind, step],
            recv_sem=row_recv.at[kind, step],
            device_id=device,
            device_id_type=MESH,
        )

    def col_copy(side, part):
        start, size = ((RR, height), (0, RR), (RR + height, RR))[part]
        if side == 0:
            src, dst, device = 1, tile_cols + 1, {"col": col - 1}
        else:
            src, dst, device = tile_cols, 0, {"col": col + 1}
        return pltpu.make_async_remote_copy(
            src_ref=grid.at[pl.ds(start, size), src],
            dst_ref=grid.at[pl.ds(start, size), dst],
            send_sem=col_send.at[side, part],
            recv_sem=col_recv.at[side, part],
            device_id=device,
            device_id_type=MESH,
        )

    def send_col(step, part):
        at = tile_col(step)

        @pl.when(jnp.logical_and(has_left, at == 0))
        def _():
            col_copy(0, part).start()

        @pl.when(jnp.logical_and(has_right, at == tile_cols - 1))
        def _():
            col_copy(1, part).start()

    @pl.loop(0, tile_cols)
    def _(step):
        for tile_row in reversed(range(tile_rows)):
            x_copy(tile_row, step).wait()
            first = jnp.logical_and(step == 0, tile_row == last)
            if tile_row == last:
                pl.when(step == 0)(reduce_copy.wait)
            x = xh.at[tile_row, step]
            hidden = jnp.dot(x[:, 0:channels], v_reduce[...], preferred_element_type=jnp.float32)
            x[:, channels:channels + mid] = jnp.maximum(hidden, 0.0).astype(jnp.bfloat16)
            if tile_row == last:
                @pl.when(step == 0)
                def _():
                    short_copy.wait()
                    expand_copy.wait()
            piece = 512
            for start in range(0, cout, piece):
                summed = jnp.dot(
                    x[...], v_cat[:, start:start + piece], preferred_element_type=jnp.float32
                )
                block[:, start:start + piece] = jnp.maximum(summed, 0.0).astype(jnp.bfloat16)
            if tile_row == last:
                pl.when(step == 0)(branch_copy.wait)
            reduced = jnp.dot(block[...], v_branch[...], preferred_element_type=jnp.float32)
            at = tile_col(step)
            kept = (codes[tile_row, at] >= 0).astype(jnp.float32)
            reduced = (jnp.maximum(reduced, 0.0) * kept).astype(jnp.bfloat16)
            grid[pl.ds(RR + tile_row * TILE, TILE), at + 1] = reduced.reshape(TILE, TILE, width)
            if tile_row == last:
                @pl.when(step == 0)
                def _():
                    total = (has_up.astype(jnp.int32) + has_down.astype(jnp.int32)
                             + has_left.astype(jnp.int32) + has_right.astype(jnp.int32))
                    pl.semaphore_wait(barrier, total)

                @pl.when(has_down)
                def _():
                    row_copy(0, step).start()

        @pl.when(has_down)
        def _():
            row_copy(1, step).start()

        @pl.when(has_up)
        def _():
            row_copy(2, step).start()

        send_col(step, 0)

    def wait_rows(step):
        @pl.when(has_up)
        def _():
            row_copy(0, step).wait_recv()
            row_copy(1, step).wait_recv()

        @pl.when(has_down)
        def _():
            row_copy(2, step).wait_recv()

    def forward(step):
        pl.when(has_up)(functools.partial(send_col, step, 1))
        pl.when(has_down)(functools.partial(send_col, step, 2))

    def wait_col(part):
        @pl.when(has_right)
        def _():
            col_copy(0, part).wait_recv()

        @pl.when(has_left)
        def _():
            col_copy(1, part).wait_recv()

    span = (tile_cols + 2) * TILE
    out_width = tile_cols * TILE

    def stack(start, count, group):
        @pl.loop(0, count // group)
        def _(index):
            first_row = start + index * group
            rows = grid[pl.ds(first_row, group)].reshape(group * span, width)
            wide = rows.astype(jnp.float32)
            size = group * span
            shift = TILE - RC
            before = pltpu.roll(wide, size - shift, 0).astype(jnp.bfloat16)
            after = pltpu.roll(wide, shift, 0).astype(jnp.bfloat16)
            here = pl.ds(first_row, group)
            stacked[here, :, 0:width] = before.reshape(group, span, width)[:, 0:out_width]
            stacked[here, :, width:2 * width] = rows.reshape(group, span, width)[:, TILE:TILE + out_width]
            stacked[here, :, 2 * width:] = after.reshape(group, span, width)[:, 2 * TILE:]

    def tap(first_row, count, down_tap):
        rows = stacked[pl.ds(first_row, count)].reshape(count * out_width, 3 * width)
        weights = v_dilated[3 * down_tap:3 * down_tap + 3].reshape(3 * width, width)
        return jnp.dot(rows, weights, preferred_element_type=jnp.float32).reshape(
            count, out_width, width
        )

    wait_rows(0)
    forward(0)
    wait_col(0)
    dilated_copy.wait()
    stack(RR, height, 2)
    inner = height - RR

    @pl.loop(0, 4)
    def _(index):
        size = height // 4
        acc[pl.ds(index * size, size)] = tap(RR + index * size, size, 1)

    @pl.loop(0, 2)
    def _(index):
        size = inner // 2
        acc[pl.ds(RR + index * size, size)] += tap(RR + index * size, size, 0)
        acc[pl.ds(index * size, size)] += tap(2 * RR + index * size, size, 2)

    for step in range(1, tile_cols):
        wait_rows(step)
        forward(step)
    pl.when(has_up)(functools.partial(wait_col, 1))
    pl.when(has_down)(functools.partial(wait_col, 2))

    def finish(start, size, taps):
        total = acc[pl.ds(start, size)]
        for down_tap in taps:
            total = total + tap(start + RR * down_tap, size, down_tap)
        out_buf[pl.ds(start, size)] = jnp.maximum(total, 0.0).astype(jnp.bfloat16)

    stack(0, RR, 2)

    @pl.loop(0, 2)
    def _(index):
        finish(index * (inner // 2), inner // 2, (0,))

    upper = pltpu.make_async_copy(out_buf.at[pl.ds(0, inner)], out.at[pl.ds(0, inner)], out_sem.at[0])
    upper.start()
    stack(RR + height, RR, 2)
    finish(inner, RR - inner, (0, 2))

    @pl.loop(0, 2)
    def _(index):
        finish(RR + index * (inner // 2), inner // 2, (2,))

    lower = pltpu.make_async_copy(out_buf.at[pl.ds(inner, RR)], out.at[pl.ds(inner, RR)], out_sem.at[1])
    lower.start()

    for step in range(tile_cols):
        @pl.when(has_down)
        def _(step=step):
            row_copy(0, step).wait_send()
            row_copy(1, step).wait_send()

        @pl.when(has_up)
        def _(step=step):
            row_copy(2, step).wait_send()

    for side, there in ((0, has_left), (1, has_right)):
        for part, other in ((0, None), (1, has_up), (2, has_down)):
            ready = there if other is None else jnp.logical_and(there, other)
            pl.when(ready)(col_copy(side, part).wait_send)
    upper.wait()
    lower.wait()


def shards(row_count, col_count, features, assignment, w_reduce, w_expand, w_short, w_branch, w_dilated):
    tile_rows, tile_cols, pixels, channels = features.shape
    mid = w_reduce.shape[1]
    cout = w_expand.shape[1]
    width = w_branch.shape[1]
    height = tile_rows * TILE
    out_width = tile_cols * TILE
    bf16 = jnp.bfloat16
    any_spec = pl.BlockSpec(memory_space=pl.ANY)
    per_pixel = channels * mid + (channels + mid) * cout + cout * width + 9 * width * width
    return pl.pallas_call(
        functools.partial(kernel, row_count, col_count),
        out_shape=jax.ShapeDtypeStruct((height, out_width, width), bf16),
        in_specs=[pl.BlockSpec(memory_space=pltpu.SMEM)] + [any_spec] * 6,
        out_specs=any_spec,
        scratch_shapes=[
            pltpu.VMEM((tile_rows, tile_cols, pixels, channels + mid), bf16),
            pltpu.VMEM((channels, mid), bf16),
            pltpu.VMEM((channels + mid, cout), bf16),
            pltpu.VMEM((cout, width), bf16),
            pltpu.VMEM(w_dilated.shape, bf16),
            pltpu.VMEM((pixels, cout), bf16),
            pltpu.VMEM((height + 2 * RR, tile_cols + 2, TILE, width), bf16),
            pltpu.VMEM((height + 2 * RR, out_width, 3 * width), bf16),
            pltpu.VMEM((height, out_width, width), jnp.float32),
            pltpu.VMEM((height, out_width, width), bf16),
            pltpu.SemaphoreType.DMA((tile_rows, tile_cols)),
            pltpu.SemaphoreType.DMA((5,)),
            pltpu.SemaphoreType.DMA((2,)),
            pltpu.SemaphoreType.DMA((3, tile_cols)),
            pltpu.SemaphoreType.DMA((3, tile_cols)),
            pltpu.SemaphoreType.DMA((2, 3)),
            pltpu.SemaphoreType.DMA((2, 3)),
        ],
        cost_estimate=pl.CostEstimate(
            flops=2 * height * out_width * per_pixel, bytes_accessed=15 * 2 ** 20, transcendentals=0
        ),
        compiler_params=pltpu.CompilerParams(
            collective_id=0, has_side_effects=True, vmem_limit_bytes=56 * 2 ** 20
        ),
    )(assignment, features, w_reduce, w_expand, w_short, w_branch, w_dilated)


def solution(mesh):
    in_specs = (
        P(("groups", "row"), "col", None, None),
        P(("groups", "row"), "col"),
        P(),
        P(),
        P(),
        P(),
        P(),
    )
    out_specs = P(("groups", "row"), "col", None)
    return jax.shard_map(
        functools.partial(shards, mesh.shape["row"], mesh.shape["col"]),
        mesh=mesh, in_specs=in_specs, out_specs=out_specs, check_vma=False,
    )
```

time: 79.8 us -> 40.6 us (0.51)
  Pallas kernels: 0 us -> 38.1 us
  matrix products: 35.3 us -> 0 us
  waiting for transfers between devices: 25.7 us -> 0 us
  starting transfers between devices: 10.6 us -> 0 us
  other arithmetic: 3.25 us -> 0 us
  local copies, waits for them, and re-layouts: 4.53 us -> 2.3 us
    pallas_call x0 -> x1, Pallas kernels: none -> 38.1 us  [shards(): pl.pallas_call(functools.partial(kernel, row_count, col_count), out_shape...]
    dot_general x3 -> x0, matrix products: 35.3 us -> none  [the longest x1 19.7 us: trunk(): jnp.dot(block_out, w_branch, preferred_element_type=jnp.float32)]
    ppermute x4 -> x0, waiting for transfers between devices: 25.7 us -> none  [the longest x2 14.8 us: extended_2(): lax.ppermute(head, axis, [((i + 1) % count, i) for i in range(ends)])]
    ppermute x4 -> x0, starting transfers between devices: 10.6 us -> none  [the longest x2 6.15 us: extended_2(): lax.ppermute(head, axis, [((i + 1) % count, i) for i in range(ends)])]
    concatenate x3 -> x0, other arithmetic: 2.27 us -> none  [extended_2(): jnp.concatenate([lax.ppermute(tail, axis, [(i, (i + 1) % count) for i in...]
    slice x4 -> x0, local copies, waits for them, and re-layouts: 1.95 us -> none  [the longest x1 1.5 us: shards(): extended[down_tap * RR:down_tap * RR + height, col_start:col_start + width]]
    ge x1 -> x0, other arithmetic: 0.83 us -> none  [shards(): tissue = tile_codes >= 0]
    unnamed x12 -> x1, local copies, waits for them, and re-layouts: 2.29 us -> 2.3 us
  transfers between devices with their start and end apart: 4 -> 0, of which waited for: 3 -> 0; matrix products, arithmetic and copies ran while one was open for 1% -> 0% of each run, Pallas kernels for 0% -> 0%
where the time goes in v1:
time: 40.6 us; the launch traced here: 40.4 us
  Pallas kernels  38.1 us (94%)
  local copies, waits for them, and re-layouts  2.3 us (6%)
    pallas_call x1, Pallas kernels, shards(): pl.pallas_call(functools.partial(kernel, row_count, col_count), out_shape...  38.1 us
    unnamed x1, local copies, waits for them, and re-layouts  2.3 us

profile of v1, /device:TPU:25, one launch (start us, length us, event | category | flops | bytes accessed | tf_op | source)
XLA Modules:
  0.0 40.4 jit_solution(14425136033471395221)
XLA Ops:
  0.0 38.1 %shard_map.73 = bf16[32,64,256]{2,1,0:T(8,128)(2,1)} custom-call(s32[2,4]{1,0:T(2,128)} %codes.1, bf16[2,4,256,1024]{3,2,1,0:T(8,128)(2,1)} %features.1, bf16[1024,512]{1,0:T(8,128)(2,1)} %w_reduce.1, bf16[512,2048]{1,0:T(8,128)(2,1)} %w_expand.1, bf16[1024,2048]{1,0:T(8,128)(2,1)} %w_short.1, bf16[2048,256]{1,0:T(8,128)(2,1)} %w_branch.1, ...), custom_call_target="tpu_custom_call" | custom-call | flops 19595788288 | bytes 15728640 | tf_op jit(solution)/shard_map/pallas_call | solution.py:304
  38.1 2.3 %copy.9 = bf16[32,64,256]{2,1,0:T(8,128)(2,1)} copy(bf16[32,64,256]{2,1,0:T(8,128)(2,1)} %shard_map.73) | data formatting | bytes 2097152

commit v2 on v1

--- a/solution.py
+++ b/solution.py
@@ -10,6 +10,7 @@
 TILE = 16
 RR = 18
 RC = 15
+PIECE = 512
 MESH = pl.DeviceIdType.MESH
 
 
@@ -17,7 +18,7 @@
     row_count, col_count,
     codes, features, w_reduce, w_expand, w_short, w_branch, w_dilated, out,
     xh, v_reduce, v_cat, v_branch, v_dilated, block, grid, stacked, acc, out_buf,
-    x_sem, w_sem, out_sem, row_send, row_recv, col_send, col_recv,
+    x_sem, w_sem, cat_sem, out_sem, row_send, row_recv, col_send, col_recv,
 ):
     tile_rows, tile_cols, pixels, channels = features.shape
     mid = w_reduce.shape[1]
@@ -45,21 +46,24 @@
 
     last = tile_rows - 1
     reduce_copy = pltpu.make_async_copy(w_reduce, v_reduce, w_sem.at[0])
-    short_copy = pltpu.make_async_copy(w_short, v_cat.at[pl.ds(0, channels)], w_sem.at[1])
-    expand_copy = pltpu.make_async_copy(w_expand, v_cat.at[pl.ds(channels, mid)], w_sem.at[2])
-    branch_copy = pltpu.make_async_copy(w_branch, v_branch, w_sem.at[3])
-    dilated_copy = pltpu.make_async_copy(w_dilated, v_dilated, w_sem.at[4])
+
+    def cat_copies(piece):
+        columns = pl.ds(piece * PIECE, PIECE)
+        return [
+            pltpu.make_async_copy(
+                part.at[:, columns], v_cat.at[pl.ds(first, part.shape[0]), columns], cat_sem.at[at, piece]
+            )
+            for at, (part, first) in enumerate(((w_short, 0), (w_expand, channels)))
+        ]
+
+    branch_copy = pltpu.make_async_copy(w_branch, v_branch, w_sem.at[1])
+    dilated_copy = pltpu.make_async_copy(w_dilated, v_dilated, w_sem.at[2])
     x_copy(last, 0).start()
     reduce_copy.start()
-    short_copy.start()
-    expand_copy.start()
+    for piece in range(cout // PIECE):
+        for copy in cat_copies(piece):
+            copy.start()
     branch_copy.start()
-    for tile_row in reversed(range(last)):
-        x_copy(tile_row, 0).start()
-    for step in range(1, tile_cols):
-        for tile_row in reversed(range(tile_rows)):
-            x_copy(tile_row, step).start()
-    dilated_copy.start()
 
     barrier = pltpu.get_barrier_semaphore()
     for there, device in sides:
@@ -132,25 +136,32 @@
     def _(step):
         for tile_row in reversed(range(tile_rows)):
             x_copy(tile_row, step).wait()
-            first = jnp.logical_and(step == 0, tile_row == last)
             if tile_row == last:
                 pl.when(step == 0)(reduce_copy.wait)
             x = xh.at[tile_row, step]
             hidden = jnp.dot(x[:, 0:channels], v_reduce[...], preferred_element_type=jnp.float32)
             x[:, channels:channels + mid] = jnp.maximum(hidden, 0.0).astype(jnp.bfloat16)
+            for piece in range(cout // PIECE):
+                if tile_row == last:
+                    @pl.when(step == 0)
+                    def _(piece=piece):
+                        for copy in cat_copies(piece):
+                            copy.wait()
+                columns = slice(piece * PIECE, (piece + 1) * PIECE)
+                summed = jnp.dot(x[...], v_cat[:, columns], preferred_element_type=jnp.float32)
+                block[:, columns] = jnp.maximum(summed, 0.0).astype(jnp.bfloat16)
             if tile_row == last:
                 @pl.when(step == 0)
                 def _():
-                    short_copy.wait()
-                    expand_copy.wait()
-            piece = 512
-            for start in range(0, cout, piece):
-                summed = jnp.dot(
-                    x[...], v_cat[:, start:start + piece], preferred_element_type=jnp.float32
-                )
-                block[:, start:start + piece] = jnp.maximum(summed, 0.0).astype(jnp.bfloat16)
-            if tile_row == last:
-                pl.when(step == 0)(branch_copy.wait)
+                    branch_copy.wait()
+                    for other in reversed(range(last)):
+                        x_copy(other, 0).start()
+                    dilated_copy.start()
+
+                @pl.when(step < tile_cols - 1)
+                def _():
+                    for other in reversed(range(tile_rows)):
+                        x_copy(other, step + 1).start()
             reduced = jnp.dot(block[...], v_branch[...], preferred_element_type=jnp.float32)
             at = tile_col(step)
             kept = (codes[tile_row, at] >= 0).astype(jnp.float32)
@@ -253,7 +264,7 @@
         total = acc[pl.ds(start, size)]
         for down_tap in taps:
             total = total + tap(start + RR * down_tap, size, down_tap)
-        out_buf[pl.ds(start, size)] = jnp.maximum(total, 0.0).astype(jnp.bfloat16)
+        out_buf[pl.ds(start, size)] = total.astype(jnp.bfloat16)
 
     stack(0, RR, 2)
 
@@ -301,7 +312,7 @@
     bf16 = jnp.bfloat16
     any_spec = pl.BlockSpec(memory_space=pl.ANY)
     per_pixel = channels * mid + (channels + mid) * cout + cout * width + 9 * width * width
-    return pl.pallas_call(
+    summed = pl.pallas_call(
         functools.partial(kernel, row_count, col_count),
         out_shape=jax.ShapeDtypeStruct((height, out_width, width), bf16),
         in_specs=[pl.BlockSpec(memory_space=pltpu.SMEM)] + [any_spec] * 6,
@@ -318,7 +329,8 @@
             pltpu.VMEM((height, out_width, width), jnp.float32),
             pltpu.VMEM((height, out_width, width), bf16),
             pltpu.SemaphoreType.DMA((tile_rows, tile_cols)),
-            pltpu.SemaphoreType.DMA((5,)),
+            pltpu.SemaphoreType.DMA((3,)),
+            pltpu.SemaphoreType.DMA((2, cout // PIECE)),
             pltpu.SemaphoreType.DMA((2,)),
             pltpu.SemaphoreType.DMA((3, tile_cols)),
             pltpu.SemaphoreType.DMA((3, tile_cols)),
@@ -329,9 +341,10 @@
             flops=2 * height * out_width * per_pixel, bytes_accessed=15 * 2 ** 20, transcendentals=0
         ),
         compiler_params=pltpu.CompilerParams(
-            collective_id=0, has_side_effects=True, vmem_limit_bytes=56 * 2 ** 20
+            collective_id=0, has_side_effects=True, vmem_limit_bytes=52 * 2 ** 20
         ),
     )(assignment, features, w_reduce, w_expand, w_short, w_branch, w_dilated)
+    return jnp.maximum(summed, jnp.zeros((), bf16))
 
 
 def solution(mesh):

time: 40.6 us -> 41.5 us (1.022)
  the two profiles are of different devices: /device:TPU:25 before, /device:TPU:0 now
where the time goes in v2:
time: 41.5 us; the launch traced here: 41.3 us
  Pallas kernels  39.6 us (95%)
  other arithmetic  1.04 us (3%)
  local copies, waits for them, and re-layouts  0.68 us (2%)
    pallas_call x1, Pallas kernels, shards(): pl.pallas_call(functools.partial(kernel, row_count, col_count), out_shape...  39.6 us
    max x1, other arithmetic, shards(): return jnp.maximum(summed, jnp.zeros((), bf16))  1.04 us

profile of v2, /device:TPU:0, one launch (start us, length us, event | category | flops | bytes accessed | tf_op | source)
XLA Modules:
  0.0 41.3 jit_solution(7344099904652252499)
XLA Ops:
  0.0 0.0 copy-start
  0.0 0.7 %copy-done = s32[2,4]{1,0:T(2,128)S(1)} copy-done((s32[2,4]{1,0:T(2,128)S(1)}, s32[2,4]{1,0:T(2,128)}, u32[]{:S(2)}) %copy-start) | copy-done | bytes 56
  0.7 39.6 %shard_map.73 = bf16[32,64,256]{2,1,0:T(8,128)(2,1)S(1)} custom-call(s32[2,4]{1,0:T(2,128)S(1)} %copy-done, bf16[2,4,256,1024]{3,2,1,0:T(8,128)(2,1)} %features.1, bf16[1024,512]{1,0:T(8,128)(2,1)} %w_reduce.1, bf16[512,2048]{1,0:T(8,128)(2,1)} %w_expand.1, bf16[1024,2048]{1,0:T(8,128)(2,1)} %w_short.1, bf16[2048,256]{1,0:T(8,128)(2,1)} %w_branch.1, ...), custom_call_target="tpu_custom_call" | custom-call | flops 19595788288 | bytes 15728640 | tf_op jit(solution)/shard_map/pallas_call | solution.py:315
  40.3 1.0 %broadcast_maximum_fusion = bf16[32,64,256]{2,1,0:T(8,128)(2,1)} fusion(bf16[32,64,256]{2,1,0:T(8,128)(2,1)S(1)} %shard_map.73), kind=kLoop, calls=%fused_computation | loop fusion | flops 524288 | bytes 2097152 | tf_op jit(solution)/shard_map/max | solution.py:347
Async XLA Ops:
  0.0 0.7 %copy-start = (s32[2,4]{1,0:T(2,128)S(1)}, s32[2,4]{1,0:T(2,128)}, u32[]{:S(2)}) copy-start(s32[2,4]{1,0:T(2,128)} %codes.1) | copy-start | bytes 100

commit v3 on v1

--- a/solution.py
+++ b/solution.py
@@ -177,19 +177,18 @@
 
         send_col(step, 0)
 
-    def wait_rows(step):
+    def wait_above(step):
         @pl.when(has_up)
         def _():
             row_copy(0, step).wait_recv()
             row_copy(1, step).wait_recv()
-
+            send_col(step, 1)
+
+    def wait_below(step):
         @pl.when(has_down)
         def _():
             row_copy(2, step).wait_recv()
-
-    def forward(step):
-        pl.when(has_up)(functools.partial(send_col, step, 1))
-        pl.when(has_down)(functools.partial(send_col, step, 2))
+            send_col(step, 2)
 
     def wait_col(part):
         @pl.when(has_right)
@@ -225,8 +224,8 @@
             count, out_width, width
         )
 
-    wait_rows(0)
-    forward(0)
+    wait_above(0)
+    wait_below(0)
     wait_col(0)
     dilated_copy.wait()
     stack(RR, height, 2)
@@ -244,16 +243,14 @@
         acc[pl.ds(index * size, size)] += tap(2 * RR + index * size, size, 2)
 
     for step in range(1, tile_cols):
-        wait_rows(step)
-        forward(step)
+        wait_above(step)
     pl.when(has_up)(functools.partial(wait_col, 1))
-    pl.when(has_down)(functools.partial(wait_col, 2))
 
     def finish(start, size, taps):
         total = acc[pl.ds(start, size)]
         for down_tap in taps:
             total = total + tap(start + RR * down_tap, size, down_tap)
-        out_buf[pl.ds(start, size)] = jnp.maximum(total, 0.0).astype(jnp.bfloat16)
+        out_buf[pl.ds(start, size)] = total.astype(jnp.bfloat16)
 
     stack(0, RR, 2)
 
@@ -263,6 +260,9 @@
 
     upper = pltpu.make_async_copy(out_buf.at[pl.ds(0, inner)], out.at[pl.ds(0, inner)], out_sem.at[0])
     upper.start()
+    for step in range(1, tile_cols):
+        wait_below(step)
+    pl.when(has_down)(functools.partial(wait_col, 2))
     stack(RR + height, RR, 2)
     finish(inner, RR - inner, (0, 2))
 
@@ -301,7 +301,7 @@
     bf16 = jnp.bfloat16
     any_spec = pl.BlockSpec(memory_space=pl.ANY)
     per_pixel = channels * mid + (channels + mid) * cout + cout * width + 9 * width * width
-    return pl.pallas_call(
+    summed = pl.pallas_call(
         functools.partial(kernel, row_count, col_count),
         out_shape=jax.ShapeDtypeStruct((height, out_width, width), bf16),
         in_specs=[pl.BlockSpec(memory_space=pltpu.SMEM)] + [any_spec] * 6,
@@ -329,9 +329,10 @@
             flops=2 * height * out_width * per_pixel, bytes_accessed=15 * 2 ** 20, transcendentals=0
         ),
         compiler_params=pltpu.CompilerParams(
-            collective_id=0, has_side_effects=True, vmem_limit_bytes=56 * 2 ** 20
+            collective_id=0, has_side_effects=True, vmem_limit_bytes=52 * 2 ** 20
         ),
     )(assignment, features, w_reduce, w_expand, w_short, w_branch, w_dilated)
+    return jnp.maximum(summed, jnp.zeros((), bf16))
 
 
 def solution(mesh):

time: 40.6 us -> 39.3 us (0.968)
  the two profiles are of different devices: /device:TPU:25 before, /device:TPU:5 now
where the time goes in v3:
time: 39.3 us; the launch traced here: 39.2 us
  Pallas kernels  37.4 us (95%)
  other arithmetic  1.04 us (3%)
  local copies, waits for them, and re-layouts  0.68 us (2%)
    pallas_call x1, Pallas kernels, shards(): pl.pallas_call(functools.partial(kernel, row_count, col_count), out_shape...  37.4 us
    max x1, other arithmetic, shards(): return jnp.maximum(summed, jnp.zeros((), bf16))  1.04 us

profile of v3, /device:TPU:5, one launch (start us, length us, event | category | flops | bytes accessed | tf_op | source)
XLA Modules:
  0.0 39.2 jit_solution(9220177920230006054)
XLA Ops:
  0.0 0.0 copy-start
  0.0 0.7 %copy-done = s32[2,4]{1,0:T(2,128)S(1)} copy-done((s32[2,4]{1,0:T(2,128)S(1)}, s32[2,4]{1,0:T(2,128)}, u32[]{:S(2)}) %copy-start) | copy-done | bytes 56
  0.7 37.4 %shard_map.73 = bf16[32,64,256]{2,1,0:T(8,128)(2,1)S(1)} custom-call(s32[2,4]{1,0:T(2,128)S(1)} %copy-done, bf16[2,4,256,1024]{3,2,1,0:T(8,128)(2,1)} %features.1, bf16[1024,512]{1,0:T(8,128)(2,1)} %w_reduce.1, bf16[512,2048]{1,0:T(8,128)(2,1)} %w_expand.1, bf16[1024,2048]{1,0:T(8,128)(2,1)} %w_short.1, bf16[2048,256]{1,0:T(8,128)(2,1)} %w_branch.1, ...), custom_call_target="tpu_custom_call" | custom-call | flops 19595788288 | bytes 15728640 | tf_op jit(solution)/shard_map/pallas_call | solution.py:304
  38.1 1.0 %broadcast_maximum_fusion = bf16[32,64,256]{2,1,0:T(8,128)(2,1)} fusion(bf16[32,64,256]{2,1,0:T(8,128)(2,1)S(1)} %shard_map.73), kind=kLoop, calls=%fused_computation | loop fusion | flops 524288 | bytes 2097152 | tf_op jit(solution)/shard_map/max | solution.py:335
Async XLA Ops:
  0.0 0.7 %copy-start = (s32[2,4]{1,0:T(2,128)S(1)}, s32[2,4]{1,0:T(2,128)}, u32[]{:S(2)}) copy-start(s32[2,4]{1,0:T(2,128)} %codes.1) | copy-start | bytes 100
